TPU v7x, 512 devices: a whole 4x8x8 slice. The times are simulated.
512 devices in a mesh: dp: 8 (over z_hi, core), lat: 64 (over x, z_lo, y).
Axes of the slice: x: 4, y: 8, z: 8 (z_hi: 4, z_lo: 2; z = z_hi * 2 + z_lo), core: 2. Of those that a mesh axis runs over, the one named last changes fastest.
Arguments:
- query_feats: bfloat16 [8, 128, 128, 1024], P('dp', 'lat'), may hold values from -32 to 32
- key_feats: bfloat16 [8, 128, 128, 1024], P('dp', 'lat'), may hold values from -6 to 6
- value_feats: bfloat16 [8, 128, 128, 1024], P('dp', 'lat'), may hold values from -6 to 6
- out_grad: bfloat16 [8, 128, 128, 1024], P('dp', 'lat'), may hold values from -6 to 6
- out_proj: bfloat16 [1024, 1024], P('lat'), may hold values from -0.1875 to 0.1875
- cycle_lo: int32 [128], replicated, may hold values from 0 to 125, as said below
- cycle_hi: int32 [128], replicated, may hold values from 2 to 127, as said below
- lon_half: int32 [128], replicated, may hold values from 1 to 64, as said below
Outputs:
- query_grad: bfloat16 [8, 128, 128, 1024], P('dp', 'lat')
- key_grad: bfloat16 [8, 128, 128, 1024], P('dp', 'lat')
- value_grad: bfloat16 [8, 128, 128, 1024], P('dp', 'lat')
- proj_grad: float32 [1024, 1024], P('lat')
Inputs may be any that keep to these rules, and one draw needn't show every extreme that they name: cycle_lo[i] is i minus 1 to 2, not below 0; within 4 cycles of either pole it is max(i - 2, 0). cycle_hi[i] is i plus 1 to 2, not above 127; within 4 cycles of either pole it is min(i + 2, 127). `lon_half`: 64, the whole cycle, within 4 cycles of either pole; at most 32 elsewhere.
All inputs are finite; a program needn't handle non-finite values.
Results may differ from a plain program's by a relative error of at most 0.015.
Values may be sent and summed in bfloat16 or wider, within the bound.
No kernel may reach another device: no remote copies, remote signals or barrier semaphores. Data moves between devices by JAX's collectives and lax.ppermute only.
A program may use at most 192 MiB of HBM per device.

v0:
```python
import math
import jax
import jax.numpy as jnp
from jax import lax
from jax.sharding import PartitionSpec as P

HEADS = 16
HEAD_DIM = 64
REACH = 2


def padded(value, sides, width):
    for axis, dim in sides:
        size, length = (lax.axis_size(axis), value.shape[dim])
        up = [(i, (i + 1) % size) for i in range(size - 1)]
        down = [(j, i) for i, j in up]
        last = lax.slice_in_dim(value, length - width, length, axis=dim)
        first = lax.slice_in_dim(value, 0, width, axis=dim)
        before = lax.ppermute(last, axis, up)
        after = lax.ppermute(first, axis, down)
        value = jnp.concatenate([before, value, after], axis=dim)
    return value


def shifted(value, axis, by):
    size = lax.axis_size(axis)
    pairs = [(i, i + by) for i in range(size) if 0 <= i + by < size]
    return lax.ppermute(value, axis, pairs)


def cycle_log_weight(cycles, total):
    latitude = (cycles.astype(jnp.float32) + 0.5) * (math.pi / total)
    return jnp.log(jnp.sin(latitude))


def attend(query_heads, key_heads, value_heads, grad_heads, allowed, log_weight):
    scaling = 1.0 / math.sqrt(HEAD_DIM)
    scores = (
        jnp.einsum("qhd,khd->hqk", query_heads, key_heads, preferred_element_type=jnp.float32)
        * scaling
    )
    scores = scores + log_weight[None, None, :]
    scores = jnp.where(allowed[None], scores, -jnp.inf)
    row_peak = jnp.max(scores, axis=-1, keepdims=True)
    unnormed = jnp.exp(scores - row_peak)
    attention = unnormed / jnp.sum(unnormed, axis=-1, keepdims=True)
    attention_low = attention.astype(jnp.bfloat16)
    attended = jnp.einsum(
        "hqk,khd->qhd", attention_low, value_heads, preferred_element_type=jnp.float32
    ).astype(jnp.bfloat16)
    row_dot = jnp.sum(grad_heads.astype(jnp.float32) * attended.astype(jnp.float32), axis=-1)
    prob_grad = jnp.einsum(
        "qhd,khd->hqk", grad_heads, value_heads, preferred_element_type=jnp.float32
    )
    score_grad = (attention * (prob_grad - row_dot.T[:, :, None]) * scaling).astype(jnp.bfloat16)
    query_part = jnp.einsum(
        "hqk,khd->qhd", score_grad, key_heads, preferred_element_type=jnp.float32
    )
    key_part = jnp.einsum(
        "hqk,qhd->khd", score_grad, query_heads, preferred_element_type=jnp.float32
    )
    value_part = jnp.einsum(
        "hqk,qhd->khd", attention_low, grad_heads, preferred_element_type=jnp.float32
    )
    return (attended, query_part, key_part, value_part)


def split_heads(matrix, groups):
    count = matrix.shape[0]
    return jnp.moveaxis(matrix.reshape(count, groups, HEADS // groups, HEAD_DIM), 1, 0)


def join_heads(stacked):
    groups, count, per_group, head_size = stacked.shape
    return jnp.moveaxis(stacked, 0, 1).reshape(count, groups * per_group * head_size)


def local(query_feats, key_feats, value_feats, out_grad, out_proj, cycle_lo, cycle_hi, lon_half):
    cycles_here = query_feats.shape[1]
    lon_count = query_feats.shape[2]
    width = query_feats.shape[3]
    query_rows = cycles_here * lon_count
    grad_flat = out_grad.reshape(query_rows, width)
    attn_grad = jnp.dot(
        grad_flat,
        lax.all_gather(out_proj, "lat", axis=0, tiled=True).T,
        preferred_element_type=jnp.float32,
    ).astype(jnp.bfloat16)
    total_cycles = cycle_lo.shape[0]
    first_cycle = lax.axis_index("lat") * cycles_here
    longitude = jnp.arange(lon_count, dtype=jnp.int32)
    lon_gap = jnp.abs(longitude[:, None] - longitude[None, :])
    lon_dist = jnp.minimum(lon_gap, lon_count - lon_gap)
    groups = HEADS // 4
    stacked = jnp.stack([key_feats[0], value_feats[0]])
    extended = padded(stacked, (("lat", 1),), REACH)
    ext_cycles = cycles_here + 2 * REACH
    key_count = ext_cycles * lon_count
    lower = lax.dynamic_slice_in_dim(cycle_lo, first_cycle, cycles_here)
    upper = lax.dynamic_slice_in_dim(cycle_hi, first_cycle, cycles_here)
    half = lax.dynamic_slice_in_dim(lon_half, first_cycle, cycles_here)
    cycle_ids = first_cycle - REACH + jnp.arange(ext_cycles, dtype=jnp.int32)
    cycle_ok = (cycle_ids[None, :] >= lower[:, None]) & (cycle_ids[None, :] <= upper[:, None])
    lon_ok = lon_dist[None, :, :] <= half[:, None, None]
    allowed = (cycle_ok[:, None, :, None] & lon_ok[:, :, None, :]).reshape(query_rows, key_count)
    cycle_weight = cycle_log_weight(jnp.clip(cycle_ids, 0, total_cycles - 1), total_cycles)
    log_weight = jnp.broadcast_to(cycle_weight[:, None], (ext_cycles, lon_count)).reshape(key_count)
    inputs = (
        split_heads(query_feats.reshape(query_rows, width), groups),
        split_heads(extended[0].reshape(key_count, width), groups),
        split_heads(extended[1].reshape(key_count, width), groups),
        split_heads(attn_grad, groups),
    )

    def per_group(items):
        return attend(items[0], items[1], items[2], items[3], allowed, log_weight)

    attended, query_part, key_part, value_part = lax.map(per_group, inputs)
    attended = join_heads(attended)
    query_part = join_heads(query_part)
    grads = jnp.stack([join_heads(key_part), join_heads(value_part)]).reshape(
        2, ext_cycles, lon_count, width
    )
    low_rim = grads[:, :REACH]
    high_rim = grads[:, REACH + cycles_here :]
    own = grads[:, REACH : REACH + cycles_here]
    from_below = shifted(high_rim.astype(jnp.bfloat16), "lat", 1).astype(high_rim.dtype)
    from_above = shifted(low_rim.astype(jnp.bfloat16), "lat", -1).astype(low_rim.dtype)
    own = own + from_below
    own = own + from_above
    query_grad = query_part.astype(jnp.bfloat16).reshape(1, cycles_here, lon_count, width)
    key_grad = own[0].astype(jnp.bfloat16)[None]
    value_grad = own[1].astype(jnp.bfloat16)[None]
    scaling = 1.0 / math.sqrt(lax.axis_size("dp") * total_cycles * lon_count)
    band_rows = lax.psum_scatter(
        jnp.dot(attended.T, grad_flat, preferred_element_type=jnp.float32),
        "lat",
        scatter_dimension=0,
        tiled=True,
    )
    summed = lax.psum(band_rows.astype(jnp.bfloat16), "dp").astype(jnp.float32)
    proj_grad = summed * scaling
    return (query_grad, key_grad, value_grad, proj_grad)


def solution(mesh):
    placed = (
        P("dp", "lat", None, None),
        P("dp", "lat", None, None),
        P("dp", "lat", None, None),
        P("dp", "lat", None, None),
        P("lat", None),
        P(),
        P(),
        P(),
    )
    return jax.shard_map(
        local,
        mesh=mesh,
        in_specs=placed,
        out_specs=(
            P("dp", "lat", None, None),
            P("dp", "lat", None, None),
            P("dp", "lat", None, None),
            P("lat", None),
        ),
        check_vma=False,
    )
```

profile of v0, /device:TPU:1, one launch (start us, length us, event | category | flops | bytes accessed | tf_op | source)
XLA Modules:
  0.0 724.8 jit_solution(13180394751480178918)
XLA Ops:
  10.1 1.3 collective-permute-start.1
  11.4 5.7 collective-permute-start
  19.3 1.3 copy.20
  21.2 10.0 %collective-permute-done.1 = bf16[2,2,128,1024]{3,2,1,0:T(8,128)(2,1)} collective-permute-done((bf16[2,2,128,1024]{3,2,1,0:T(8,128)(2,1)S(1)}, bf16[2,2,128,1024]{3,2,1,0:T(8,128)(2,1)}, u32[]{:S(2)}, u32[]{:S(2)}) %collective-permute-start.1) | collective-permute-done | bytes 1048608 | tf_op jit(solution)/shard_map/ppermute | solution.py:20
  32.4 1.7 pad_maximum_fusion
  34.1 2.1 fusion.61
  36.2 3.2 copy.21
  39.5 2.7 reshape_reshape_squeeze.7
  42.2 3.2 copy.19
  45.4 2.8 reshape_reshape_squeeze.6
  48.2 226.9 %all-gather.2.cloned.1.call-done = bf16[1024,1024]{1,0:T(8,128)(2,1)} async-done(((bf16[16,1024]{1,0:T(8,128)(2,1)}), bf16[1024,1024]{1,0:T(8,128)(2,1)}) %all-gather.2.cloned.1.call-update) | async-done | bytes 2097168 | tf_op jit(solution)/shard_map/all_gather | solution.py:86
  275.2 3.1 convolution_convert_fusion.1
  278.3 1.2 copy.22
  279.5 44.8 %while.17 = (s32[]{:T(128)}, bf16[4,256,4,64]{1,3,2,0:T(8,128)(2,1)}, bf16[4,256,4,64]{1,3,2,0:T(8,128)(2,1)}, f32[4,768,4,64]{1,3,2,0:T(8,128)}, f32[4,768,4,64...) while((s32[]{:T(128)}, ...), condition=%wide.region_4.5_spmd.clone, body=%wide.region_0.4_spmd.clone.sunk | while | flops 613940992 | bytes 47252764 | solution.py:118
  279.9 2.9 fusion.99
  282.9 2.3 fusion.100
  285.2 1.3 bitcast_dynamic-update-slice_fusion.2
  288.2 1.3 fusion.102
  289.5 1.3 fusion.103
  291.2 2.9 fusion.99
  294.1 2.3 fusion.100
  296.4 1.2 bitcast_dynamic-update-slice_fusion.2
  299.4 1.3 fusion.102
  300.7 1.3 fusion.103
  302.4 2.9 fusion.99
  305.3 2.3 fusion.100
  307.6 1.3 bitcast_dynamic-update-slice_fusion.2
  310.6 1.3 fusion.102
  311.9 1.3 fusion.103
  313.6 2.9 fusion.99
  316.5 2.3 fusion.100
  318.8 1.3 bitcast_dynamic-update-slice_fusion.2
  321.8 1.3 fusion.102
  323.1 1.3 fusion.103
  324.4 3.7 fusion.63
  328.1 4.6 stack.12
  332.7 4.6 stack.11
  337.3 2.6 constant_dynamic-update-slice_fusion.3
  341.8 2.5 copy-done.2
  344.3 2.5 fusion.60
  346.7 1.5 collective-permute-start.2
  348.2 1.5 collective-permute-start.3
  349.7 1.2 convert_element_type.66
  352.0 8.2 %collective-permute-done.2 = bf16[2,2,128,1024]{2,1,3,0:T(2,128)(2,1)S(1)} collective-permute-done((bf16[2,2,128,1024]{2,1,3,0:T(2,128)(2,1)}, bf16[2,2,128,1024]{2,1,3,0:T(2,128)(2,1)S(1)}, u32[]{:S(2)}, u32[]{:S(2)}) %collective-permute-start.2) | collective-permute-done | bytes 1048608 | tf_op jit(solution)/shard_map/ppermute | solution.py:28
  360.2 3.8 collective-permute-done.3
  364.0 4.5 fusion.54
  371.4 273.1 %reduce-scatter.2.cloned.1.call-done = f32[16,1024]{1,0:T(8,128)} async-done(((f32[1024,1024]{1,0:T(8,128)}), f32[16,1024]{1,0:T(8,128)}) %reduce-scatter.2.cloned.1.call-update) | async-done | bytes 65552 | tf_op jit(solution)/shard_map/reduce_scatter | solution.py:135
  645.4 71.9 %psum.7 = bf16[16,1024]{1,0:T(8,128)(2,1)S(1)} all-reduce(bf16[16,1024]{1,0:T(8,128)(2,1)S(1)} %convert_element_type.69), channel_id=1, replica_groups=mesh['dp'=8,'lat'=64] {'dp'}, use_global_device_ids=true, to_apply=%region_6.7 | all-reduce | flops 16384 | bytes 65536 | tf_op jit(solution)/shard_map/psum | solution.py:141
  (91 shorter events, 22.7 us)
Async XLA Ops:
  7.2 268.0 %copy-start = (bf16[1,2,128,1024]{3,2,1,0:T(8,128)(2,1)S(1)}, bf16[1,2,128,1024]{3,2,1,0:T(8,128)(2,1)}, u32[]{:S(2)}) copy-start(bf16[1,2,128,1024]{3,2,1,0:T(8,128)(2,1)} %param.13) | copy-start | bytes 1572868
  7.2 268.0 %all-gather.2.cloned.1.call-start = ((), (), s32[]{:S(2)}) async-start(), calls=%async_computation.1 | async-start | bytes 2129920 | tf_op jit(solution)/shard_map/all_gather | solution.py:86
  7.9 636.6 %reduce-scatter.2.cloned.1.call-start = ((), (), s32[]{:S(2)}) async-start(), calls=%async_computation.2 | async-start | bytes 4259840 | tf_op jit(solution)/shard_map/reduce_scatter | solution.py:135
  10.1 21.1 %collective-permute-start.1 = (bf16[2,2,128,1024]{3,2,1,0:T(8,128)(2,1)S(1)}, bf16[2,2,128,1024]{3,2,1,0:T(8,128)(2,1)}, u32[]{:S(2)}, u32[]{:S(2)}) collective-permute-start(bf16[2,2,128,1024]{3,2,1,0:T(8,128)(2,1)S(1)} %constant_dynamic-update-slice_fusion), channel_id=1, source_target_pairs={{1,0},{2,1},{3,2},{4,3},{5,4},{6,5},{7,6},{8,7},{9,8},{10,9},{11,1... | collective-permute-start | bytes 3145736 | tf_op jit(solution)/shard_map/ppermute | solution.py:20
  11.4 21.0 %collective-permute-start = (bf16[2,2,128,1024]{3,2,1,0:T(8,128)(2,1)S(1)}, bf16[2,2,128,1024]{3,2,1,0:T(8,128)(2,1)}, u32[]{:S(2)}, u32[]{:S(2)}) collective-permute-start(bf16[2,2,128,1024]{3,2,1,0:T(8,128)(2,1)S(1)} %constant_dynamic-update-slice_fusion), channel_id=1, source_target_pairs={{0,1},{1,2},{2,3},{3,4},{4,5},{5,6},{6,7},{7,8},{8,9},{9,10},{10,1... | collective-permute-start | bytes 3145736 | tf_op jit(solution)/shard_map/ppermute | solution.py:19
  48.2 231.3 %copy-start.4 = (bf16[768,4,4,64]{0,3,2,1:T(8,128)(2,1)S(1)}, bf16[768,4,4,64]{0,3,2,1:T(8,128)(2,1)}, u32[]{:S(2)}) copy-start(bf16[768,4,4,64]{0,3,2,1:T(8,128)(2,1)} %reshape_reshape_squeeze.7) | copy-start | bytes 4718596
  282.8 2.4 copy-start.5
  282.9 3.7 copy-start.1
  286.5 1.0 copy-start.6
  288.2 2.6 copy-start.7
  294.1 2.4 copy-start.5
  294.1 3.7 copy-start.1
  297.8 1.0 copy-start.6
  299.4 2.6 copy-start.7
  305.3 2.4 copy-start.5
  305.3 3.7 copy-start.1
  308.9 1.0 copy-start.6
  310.6 2.6 copy-start.7
  316.5 2.4 copy-start.5
  316.5 3.7 copy-start.1
  320.1 1.0 copy-start.6
  321.8 2.6 copy-start.7
  337.3 3.4 copy-start.3
  341.0 3.2 copy-start.2
  346.7 13.5 %collective-permute-start.2 = (bf16[2,2,128,1024]{2,1,3,0:T(2,128)(2,1)}, bf16[2,2,128,1024]{2,1,3,0:T(2,128)(2,1)S(1)}, u32[]{:S(2)}, u32[]{:S(2)}) collective-permute-start(bf16[2,2,128,1024]{2,1,3,0:T(2,128)(2,1)} %get-tuple-element.130), channel_id=1, source_target_pairs={{0,1},{1,2},{2,3},{3,4},{4,5},{5,6},{6,7},{7,8},{8,9},{9,10},{10,1... | collective-permute-start | bytes 3145736 | tf_op jit(solution)/shard_map/ppermute | solution.py:28
  348.2 15.8 %collective-permute-start.3 = (bf16[2,2,128,1024]{2,1,3,0:T(2,128)(2,1)}, bf16[2,2,128,1024]{2,1,3,0:T(2,128)(2,1)S(1)}, u32[]{:S(2)}, u32[]{:S(2)}) collective-permute-start(bf16[2,2,128,1024]{2,1,3,0:T(2,128)(2,1)} %get-tuple-element.131), channel_id=1, source_target_pairs={{1,0},{2,1},{3,2},{4,3},{5,4},{6,5},{7,6},{8,7},{9,8},{10,9},{11,1... | collective-permute-start | bytes 3145736 | tf_op jit(solution)/shard_map/ppermute | solution.py:28
Sparse Core Ops, SparseCore 0:
  10.1 265.0 all-gather.1
  328.3 316.2 reduce-scatter.1
where the time goes:
time: 726 us; the launch traced here: 725 us
  waiting for transfers between devices  524 us (72%)
  blocking collectives  71.9 us (10%)
  local copies, waits for them, and re-layouts  46 us (6%)
  matrix products  39.6 us (5%)
  other arithmetic  18.8 us (3%)
  between operations  14.2 us (2%)
  starting transfers between devices  9.99 us (1%)
    reduce_scatter x1, waiting for transfers between devices, local(): lax.psum_scatter(jnp.dot(attended.T, grad_flat, preferred_element_type=jn...  273 us
    all_gather x1, waiting for transfers between devices, local(): lax.all_gather(out_proj, 'lat', axis=0, tiled=True)  227 us
    psum x1, blocking collectives, local(): summed = lax.psum(band_rows.astype(jnp.bfloat16), 'dp').astype(jnp.float32)  71.9 us
  transfers between devices with their start and end apart: 6, of which 6 were waited for; matrix products, arithmetic and copies ran while one was open for 6% of the time, Pallas kernels for 0%

commit v1 on v0

--- a/solution.py
+++ b/solution.py
@@ -83,7 +83,9 @@
     grad_flat = out_grad.reshape(query_rows, width)
     attn_grad = jnp.dot(
         grad_flat,
-        lax.all_gather(out_proj, "lat", axis=0, tiled=True).T,
+        jnp.concatenate(
+            lax.all_to_all(jnp.stack([out_proj] * lax.axis_size("lat")), "lat", 0, 0), axis=0
+        ).T,
         preferred_element_type=jnp.float32,
     ).astype(jnp.bfloat16)
     total_cycles = cycle_lo.shape[0]

time: 726 us -> 522 us (0.72)
  waiting for transfers between devices: 524 us -> 307 us
  starting transfers between devices: 9.99 us -> 24.4 us
    all_gather x1 -> x0, waiting for transfers between devices: 227 us -> none  [local(): lax.all_gather(out_proj, 'lat', axis=0, tiled=True)]
    reduce_scatter x1, waiting for transfers between devices: 273 us -> 222 us  [local(): lax.psum_scatter(jnp.dot(attended.T, grad_flat, preferred_element_type=jn...]
    ppermute x1, waiting for transfers between devices: 10 us -> 60.2 us  [padded(): after = lax.ppermute(first, axis, down)]
    all_to_all x0 -> x1, starting transfers between devices: none -> 13.3 us  [local(): lax.all_to_all(jnp.stack([out_proj] * lax.axis_size('lat')), 'lat', 0, 0)]
    ppermute x2, waiting for transfers between devices: 12 us -> 24.8 us  [shifted(): return lax.ppermute(value, axis, pairs)]
  transfers between devices with their start and end apart: 6 -> 6, of which waited for: 6 -> 4; matrix products, arithmetic and copies ran while one was open for 6% -> 8% of each run, Pallas kernels for 0% -> 0%
where the time goes in v1:
time: 522 us; the launch traced here: 521 us
  waiting for transfers between devices  307 us (59%)
  blocking collectives  72.4 us (14%)
  local copies, waits for them, and re-layouts  43.4 us (8%)
  matrix products  39.7 us (8%)
  starting transfers between devices  24.4 us (5%)
  other arithmetic  18.9 us (4%)
  between operations  14.3 us (3%)
    reduce_scatter x1, waiting for transfers between devices, local(): lax.psum_scatter(jnp.dot(attended.T, grad_flat, preferred_element_type=jn...  222 us
    psum x1, blocking collectives, local(): summed = lax.psum(band_rows.astype(jnp.bfloat16), 'dp').astype(jnp.float32)  72.4 us
    ppermute x1, waiting for transfers between devices, padded(): after = lax.ppermute(first, axis, down)  60.2 us
    ppermute x2, waiting for transfers between devices, shifted(): return lax.ppermute(value, axis, pairs)  24.8 us
    all_to_all x1, starting transfers between devices, local(): lax.all_to_all(jnp.stack([out_proj] * lax.axis_size('lat')), 'lat', 0, 0)  13.3 us
    sub x4, matrix products, attend(): unnormed = jnp.exp(scores - row_peak)  11.6 us
  transfers between devices with their start and end apart: 6, of which 4 were waited for; matrix products, arithmetic and copies ran while one was open for 8% of the time, Pallas kernels for 0%

profile of v1, /device:TPU:1, one launch (start us, length us, event | category | flops | bytes accessed | tf_op | source)
XLA Modules:
  0.0 520.6 jit_solution(4090548723826978387)
XLA Ops:
  7.2 2.4 stack.11
  9.6 13.3 %all-to-all-start = ((bf16[64,16,1024]{2,1,0:T(8,128)(2,1)}), bf16[64,16,1024]{2,1,0:T(8,128)(2,1)}, u32[]{:S(2)}, u32[]{:S(2)}) async-start(bf16[64,16,1024]{2,1,0:T(8,128)(2,1)} %stack.11), calls=%async_computation | async-start | bytes 4194304 | tf_op jit(solution)/shard_map/all_to_all | solution.py:87
  23.1 1.3 collective-permute-start.1
  24.4 5.1 collective-permute-start
  30.8 60.2 %collective-permute-done.1 = bf16[2,2,128,1024]{3,2,1,0:T(8,128)(2,1)} collective-permute-done((bf16[2,2,128,1024]{3,2,1,0:T(8,128)(2,1)S(1)}, bf16[2,2,128,1024]{3,2,1,0:T(8,128)(2,1)}, u32[]{:S(2)}, u32[]{:S(2)}) %collective-permute-start.1) | collective-permute-done | bytes 1048608 | tf_op jit(solution)/shard_map/ppermute | solution.py:20
  91.0 1.7 pad_maximum_fusion
  92.7 2.0 fusion.61
  94.7 3.2 copy.21
  98.0 2.7 reshape_reshape_squeeze.7
  100.7 3.2 copy.19
  103.9 2.8 reshape_reshape_squeeze.6
  106.7 3.2 convolution_convert_fusion.1
  110.0 1.2 copy.22
  111.2 44.9 %while.17 = (s32[]{:T(128)}, bf16[4,256,4,64]{1,3,2,0:T(8,128)(2,1)}, bf16[4,256,4,64]{1,3,2,0:T(8,128)(2,1)}, f32[4,768,4,64]{1,3,2,0:T(8,128)}, f32[4,768,4,64...) while((s32[]{:T(128)}, ...), condition=%wide.region_4.5_spmd.clone, body=%wide.region_0.4_spmd.clone.sunk | while | flops 613940992 | bytes 47252764 | solution.py:120
  111.6 2.9 fusion.99
  114.5 2.3 fusion.100
  116.9 1.3 bitcast_dynamic-update-slice_fusion.2
  119.8 1.4 fusion.102
  121.2 1.3 fusion.103
  122.9 2.9 fusion.99
  125.8 2.3 fusion.100
  128.1 1.2 bitcast_dynamic-update-slice_fusion.2
  131.1 1.3 fusion.102
  132.4 1.3 fusion.103
  134.1 2.9 fusion.99
  137.0 2.3 fusion.100
  139.3 1.3 bitcast_dynamic-update-slice_fusion.2
  142.3 1.3 fusion.102
  143.6 1.3 fusion.103
  145.3 2.9 fusion.99
  148.2 2.3 fusion.100
  150.5 1.3 bitcast_dynamic-update-slice_fusion.2
  153.5 1.3 fusion.102
  154.8 1.3 fusion.103
  156.1 3.7 fusion.63
  159.8 4.6 stack.13
  164.4 4.6 stack.12
  169.0 2.6 constant_dynamic-update-slice_fusion.3
  173.5 2.5 copy-done.2
  176.0 2.5 fusion.60
  178.4 3.2 collective-permute-start.2
  181.7 1.5 collective-permute-start.3
  183.1 1.2 convert_element_type.66
  185.4 20.9 %collective-permute-done.2 = bf16[2,2,128,1024]{2,1,3,0:T(2,128)(2,1)S(1)} collective-permute-done((bf16[2,2,128,1024]{2,1,3,0:T(2,128)(2,1)}, bf16[2,2,128,1024]{2,1,3,0:T(2,128)(2,1)S(1)}, u32[]{:S(2)}, u32[]{:S(2)}) %collective-permute-start.2) | collective-permute-done | bytes 1048608 | tf_op jit(solution)/shard_map/ppermute | solution.py:28
  206.3 4.0 collective-permute-done.3
  210.3 4.5 fusion.54
  217.7 222.1 %reduce-scatter.2.cloned.1.call-done = f32[16,1024]{1,0:T(8,128)} async-done(((f32[1024,1024]{1,0:T(8,128)}), f32[16,1024]{1,0:T(8,128)}) %reduce-scatter.2.cloned.1.call-update) | async-done | bytes 65552 | tf_op jit(solution)/shard_map/reduce_scatter | solution.py:137
  440.7 72.4 %psum.7 = bf16[16,1024]{1,0:T(8,128)(2,1)S(1)} all-reduce(bf16[16,1024]{1,0:T(8,128)(2,1)S(1)} %convert_element_type.69), channel_id=1, replica_groups=mesh['dp'=8,'lat'=64] {'dp'}, use_global_device_ids=true, to_apply=%region_6.7 | all-reduce | flops 16384 | bytes 65536 | tf_op jit(solution)/shard_map/psum | solution.py:143
  (103 shorter events, 17.2 us)
Async XLA Ops:
  7.2 99.5 %copy-start = (bf16[1,2,128,1024]{3,2,1,0:T(8,128)(2,1)S(1)}, bf16[1,2,128,1024]{3,2,1,0:T(8,128)(2,1)}, u32[]{:S(2)}) copy-start(bf16[1,2,128,1024]{3,2,1,0:T(8,128)(2,1)} %param.13) | copy-start | bytes 1572868
  7.2 15.9 %copy-start.6 = (bf16[1,2,128,1024]{3,2,1,0:T(8,128)(2,1)S(1)}, bf16[1,2,128,1024]{3,2,1,0:T(8,128)(2,1)}, u32[]{:S(2)}) copy-start(bf16[1,2,128,1024]{3,2,1,0:T(8,128)(2,1)} %param.11) | copy-start | bytes 1572868
  9.6 13.5 %copy-start.7 = (bf16[1,2,128,1024]{3,2,1,0:T(8,128)(2,1)S(1)}, bf16[1,2,128,1024]{3,2,1,0:T(8,128)(2,1)}, u32[]{:S(2)}) copy-start(bf16[1,2,128,1024]{3,2,1,0:T(8,128)(2,1)} %param.12) | copy-start | bytes 1572868
  9.6 19.9 %copy-start.11 = (s32[128]{0:T(128)S(1)}, s32[128]{0:T(128)}, u32[]{:S(2)}) copy-start(s32[128]{0:T(128)} %param.15) | copy-start | bytes 1540
  9.6 20.0 %copy-start.12 = (s32[128]{0:T(128)S(1)}, s32[128]{0:T(128)}, u32[]{:S(2)}) copy-start(s32[128]{0:T(128)} %param.16) | copy-start | bytes 1540
  9.6 20.0 %copy-start.13 = (s32[128]{0:T(128)S(1)}, s32[128]{0:T(128)}, u32[]{:S(2)}) copy-start(s32[128]{0:T(128)} %param.17) | copy-start | bytes 1540
  9.6 20.1 %copy-start.8 = (bf16[1,2,128,1024]{3,2,1,0:T(8,128)(2,1)S(1)}, bf16[1,2,128,1024]{3,2,1,0:T(8,128)(2,1)}, u32[]{:S(2)}) copy-start(bf16[1,2,128,1024]{3,2,1,0:T(8,128)(2,1)} %param.10) | copy-start | bytes 1572868
  9.6 97.1 %all-to-all-start = ((bf16[64,16,1024]{2,1,0:T(8,128)(2,1)}), bf16[64,16,1024]{2,1,0:T(8,128)(2,1)}, u32[]{:S(2)}, u32[]{:S(2)}) async-start(bf16[64,16,1024]{2,1,0:T(8,128)(2,1)} %stack.11), calls=%async_computation | async-start | bytes 4194304 | tf_op jit(solution)/shard_map/all_to_all | solution.py:87
  23.0 416.9 %reduce-scatter.2.cloned.1.call-start = ((), (), s32[]{:S(2)}) async-start(), calls=%async_computation.2 | async-start | bytes 4259840 | tf_op jit(solution)/shard_map/reduce_scatter | solution.py:137
  23.1 67.8 %collective-permute-start.1 = (bf16[2,2,128,1024]{3,2,1,0:T(8,128)(2,1)S(1)}, bf16[2,2,128,1024]{3,2,1,0:T(8,128)(2,1)}, u32[]{:S(2)}, u32[]{:S(2)}) collective-permute-start(bf16[2,2,128,1024]{3,2,1,0:T(8,128)(2,1)S(1)} %constant_dynamic-update-slice_fusion), channel_id=1, source_target_pairs={{1,0},{2,1},{3,2},{4,3},{5,4},{6,5},{7,6},{8,7},{9,8},{10,9},{11,1... | collective-permute-start | bytes 3145736 | tf_op jit(solution)/shard_map/ppermute | solution.py:20
  24.4 66.5 %collective-permute-start = (bf16[2,2,128,1024]{3,2,1,0:T(8,128)(2,1)S(1)}, bf16[2,2,128,1024]{3,2,1,0:T(8,128)(2,1)}, u32[]{:S(2)}, u32[]{:S(2)}) collective-permute-start(bf16[2,2,128,1024]{3,2,1,0:T(8,128)(2,1)S(1)} %constant_dynamic-update-slice_fusion), channel_id=1, source_target_pairs={{0,1},{1,2},{2,3},{3,4},{4,5},{5,6},{6,7},{7,8},{8,9},{9,10},{10,1... | collective-permute-start | bytes 3145736 | tf_op jit(solution)/shard_map/ppermute | solution.py:19
  106.7 4.5 copy-start.4
  114.5 2.4 copy-start.5
  114.5 3.7 copy-start.1
  118.2 1.0 copy-start.9
  119.8 2.7 copy-start.10
  125.8 2.4 copy-start.5
  125.8 3.7 copy-start.1
  129.4 1.0 copy-start.9
  131.1 2.6 copy-start.10
  137.0 2.4 copy-start.5
  137.0 3.7 copy-start.1
  140.7 1.0 copy-start.9
  142.3 2.6 copy-start.10
  148.2 2.4 copy-start.5
  148.2 3.7 copy-start.1
  151.9 1.0 copy-start.9
  153.5 2.6 copy-start.10
  169.0 3.4 copy-start.3
  172.8 3.2 copy-start.2
  178.4 27.8 %collective-permute-start.2 = (bf16[2,2,128,1024]{2,1,3,0:T(2,128)(2,1)}, bf16[2,2,128,1024]{2,1,3,0:T(2,128)(2,1)S(1)}, u32[]{:S(2)}, u32[]{:S(2)}) collective-permute-start(bf16[2,2,128,1024]{2,1,3,0:T(2,128)(2,1)} %get-tuple-element.130), channel_id=1, source_target_pairs={{0,1},{1,2},{2,3},{3,4},{4,5},{5,6},{6,7},{7,8},{8,9},{9,10},{10,1... | collective-permute-start | bytes 3145736 | tf_op jit(solution)/shard_map/ppermute | solution.py:28
  181.7 28.6 %collective-permute-start.3 = (bf16[2,2,128,1024]{2,1,3,0:T(2,128)(2,1)}, bf16[2,2,128,1024]{2,1,3,0:T(2,128)(2,1)S(1)}, u32[]{:S(2)}, u32[]{:S(2)}) collective-permute-start(bf16[2,2,128,1024]{2,1,3,0:T(2,128)(2,1)} %get-tuple-element.131), channel_id=1, source_target_pairs={{1,0},{2,1},{3,2},{4,3},{5,4},{6,5},{7,6},{8,7},{9,8},{10,9},{11,1... | collective-permute-start | bytes 3145736 | tf_op jit(solution)/shard_map/ppermute | solution.py:28
Sparse Core Ops, SparseCore 0:
  159.9 279.8 reduce-scatter.1
